TPU v7x, 128 devices: a whole 4x4x4 slice. The times are simulated.
128 devices in a mesh: tm: 32 (over y, z, core), space: 4 (over x).
Axes of the slice: x: 4, y: 4, z: 4, core: 2. Of those that a mesh axis runs over, the one named last changes fastest.
Arguments:
- iterate: float32 [32, 2, 128, 1024], P('tm', None, 'space'), may hold values from -1.6 to 1.6, as said below
Outputs:
- coarse_iterate: float32 [32, 2, 128, 1024], P('tm', None, 'space')
- residual: float32 [32, 2, 128, 1024], P('tm', None, 'space')
Inputs may be any that keep to these rules, and one draw needn't show every extreme that they name: `iterate`: row 0 holds the initial condition.
All inputs are finite; a program needn't handle non-finite values.
Results may differ from a plain program's by a relative error of at most 0.00002.
Values sent between devices are 32-bit elements; how exact they have to be, the bound alone decides.
A program may use at most 64 MiB of HBM per device.

v0:
```python
import jax
import jax.numpy as jnp
from jax import lax
from jax.sharding import PartitionSpec as P

M = 16


viscosity = 0.8
time_step = 0.015625


def padded_2(shard, sides, width):
    for axis, dim in sides:
        size, length = (lax.axis_size(axis), shard.shape[dim])
        up = [(i, (i + 1) % size) for i in range(size - 1)]
        down = [(j, i) for i, j in up]
        last = lax.slice_in_dim(shard, length - width, length, axis=dim)
        initial = lax.slice_in_dim(shard, 0, width, axis=dim)
        before = lax.ppermute(last, axis, up)
        after = lax.ppermute(initial, axis, down)
        shard = jnp.concatenate([before, shard, after], axis=dim)
    return shard


def passed_along(shard, axis, by):
    size = lax.axis_size(axis)
    pairs = [(i, i + by) for i in range(size) if 0 <= i + by < size]
    return lax.ppermute(shard, axis, pairs)


def tendency(padded):
    center = padded[..., 1:-1, :]
    above = padded[..., 2:, :]
    below = padded[..., :-2, :]
    left_cells = jnp.roll(center, 1, axis=-1)
    right_cells = jnp.roll(center, -1, axis=-1)
    slope_x = 0.5 * (right_cells - left_cells)
    slope_y = 0.5 * (above - below)
    laplace = above + below + (left_cells + right_cells) - 4.0 * center
    advect = center[..., 0:1, :, :] * slope_x + center[..., 1:2, :, :] * slope_y
    return viscosity * laplace - advect


def section_mask(first_row, extent, total_rows):
    global_rows = first_row + jnp.arange(extent, dtype=jnp.int32)
    inside = (global_rows >= 0) & (global_rows < total_rows)
    return inside.astype(jnp.float32)[:, None]


def heun_padded(padded, step, first_row, total_rows):
    middle = padded[..., 1:-1, :] + step * tendency(padded)
    middle = middle * section_mask(first_row + 1, middle.shape[-2], total_rows)
    updated = 0.5 * (padded[..., 2:-2, :] + middle[..., 1:-1, :] + step * tendency(middle))
    return updated * section_mask(first_row + 2, updated.shape[-2], total_rows)


def advance_once(state, step, frame):
    base_row, total_rows = frame
    padded = padded_2(state, (("space", 2),), 2)
    return heun_padded(padded, step, base_row - 2, total_rows)


def propagate(state, steps_count, frame):
    result_state = lax.fori_loop(
        0, steps_count, lambda index, value: advance_once(value, time_step, frame), state
    )
    return result_state


def on_device(iterate):
    cells = iterate.shape[2]
    frame = (lax.axis_index("space") * cells, cells * lax.axis_size("space"))
    coarse_step = time_step * M
    relaxed = propagate(iterate, M, frame)
    moved = passed_along(relaxed, "tm", 1)
    leading = lax.axis_index("tm") == 0
    restart = jnp.concatenate([jnp.where(leading, iterate, moved), relaxed[:-1]], axis=0)
    propagated = propagate(restart, M, frame)
    residual = propagated - relaxed
    terms = propagated - advance_once(restart, coarse_step, frame)

    def local_solve(start_state):
        state = start_state
        state = advance_once(state, coarse_step, frame) + terms
        pieces = [state]
        return jnp.concatenate(pieces, axis=0)

    def one_round(index, carried):
        solved = local_solve(carried)
        passed = passed_along(solved[-1:], "tm", 1)
        return jnp.where(leading, carried, passed)

    carried = lax.fori_loop(0, lax.axis_size("tm") - 1, one_round, restart)
    coarse_iterate = local_solve(carried)
    return (coarse_iterate, residual)


def solution(mesh):
    in_specs = (P("tm", None, "space", None),)
    out_specs = (P("tm", None, "space", None), P("tm", None, "space", None))
    return jax.shard_map(
        on_device, mesh=mesh, in_specs=in_specs, out_specs=out_specs, check_vma=False
    )
```

profile of v0, /device:TPU:25, one launch (start us, length us, event | category | flops | bytes accessed | tf_op | source)
XLA Modules:
  0.0 875.4 jit_solution(5812116134673092538)
XLA Ops:
  1.6 120.4 %while.36 = (s32[]{:T(128)}, f32[1,2,32,1024]{3,2,1,0:T(8,128)S(1)}, s32[]{:T(128)}, s32[]{:T(128)}, s32[]{:T(128)}) while((s32[]{:T(128)}, f32[1,2,32,1024]{3,2,1,0:T(8,128)S(1)}, s32[]{:T(128)}, s32[]{:T(128)}, s32[]{:T(128)}) %tuple.147), condition=%wide.region_1.2_spmd, body=%wide.region_0.1_spmd.sunk | while | flops 2994508 | bytes 8649797 | solution.py:65
  122.0 22.0 %collective-permute-start.7 = (f32[1,2,32,1024]{3,2,1,0:T(8,128)S(1)}, f32[1,2,32,1024]{3,2,1,0:T(8,128)S(1)}, u32[]{:S(2)}, u32[]{:S(2)}) collective-permute-start(f32[1,2,32,1024]{3,2,1,0:T(8,128)S(1)} %get-tuple-element.162), channel_id=1, source_target_pairs={{0,4},{4,8},{8,12},{12,16},{16,20},{20,24},{24,28},{28,32},{32,36}... | collective-permute-start | bytes 786440 | tf_op jit(solution)/shard_map/ppermute | solution.py:29
  148.7 4.5 collective-permute-start.8
  155.7 121.1 %while.37 = (s32[]{:T(128)}, f32[1,2,32,1024]{3,2,1,0:T(8,128)S(1)}, s32[]{:T(128)}, s32[]{:T(128)}, s32[]{:T(128)}) while((s32[]{:T(128)}, f32[1,2,32,1024]{3,2,1,0:T(8,128)S(1)}, s32[]{:T(128)}, s32[]{:T(128)}, s32[]{:T(128)}) %tuple.146), condition=%wide.region_3.4_spmd, body=%wide.region_2.3_spmd.sunk | while | flops 2994508 | bytes 8649797 | solution.py:65
  277.8 589.1 %while.38 = (s32[]{:T(128)}, f32[1,2,32,1024]{3,2,1,0:T(8,128)S(1)}, pred[]{:T(512)}, s32[]{:T(128)}, s32[]{:T(128)}, /*index=5*/f32[1,2,32,1024]{3,2,1,0:T(8,128)S(1)}, s32[]{:T(128)}) while((s32[]{:T(128)}, f32[1,2,32,1024]{3,2,1,0:T(8,128)S(1)}, pred[]{:T(512)}, s32[]{:T(128)}, s32[]{:T(128)}, /*index=5*/f32[1,2,32,1024]{3,2,1,0:T(8,128)S(1)}, ...), condition=%wide.region_5.6_spmd, body=%wide.region_4.5_spmd.sunk | while | flops 3125580 | bytes 10747006 | solution.py:94
  285.3 23.9 %collective-permute-start.6 = (f32[1,2,32,1024]{3,2,1,0:T(8,128)S(1)}, f32[1,2,32,1024]{3,2,1,0:T(8,128)S(1)}, u32[]{:S(2)}, u32[]{:S(2)}) collective-permute-start(f32[1,2,32,1024]{3,2,1,0:T(8,128)S(1)} %multiply_add_fusion.3), channel_id=1, source_target_pairs={{0,4},{4,8},{8,12},{12,16},{16,20},{20,24},{24,28},{28,32},{32,36}... | collective-permute-start | bytes 786440 | tf_op jit(solution)/shard_map/while/body/eval_jaxpr/ppermute | solution.py:29
  313.9 4.5 collective-permute-start.5
  320.4 5.2 collective-permute-start.6
  330.7 4.5 collective-permute-start.5
  337.2 4.9 collective-permute-start.6
  342.1 5.8 collective-permute-done.6
  349.2 4.5 collective-permute-start.5
  358.5 7.9 collective-permute-done.6
  367.8 4.5 collective-permute-start.5
  376.2 8.7 collective-permute-done.6
  386.3 4.5 collective-permute-start.5
  394.7 8.7 collective-permute-done.6
  404.8 4.5 collective-permute-start.5
  413.3 8.7 collective-permute-done.6
  423.4 4.5 collective-permute-start.5
  431.8 8.7 collective-permute-done.6
  441.9 4.5 collective-permute-start.5
  450.3 8.7 collective-permute-done.6
  460.5 4.5 collective-permute-start.5
  468.9 8.7 collective-permute-done.6
  479.0 4.5 collective-permute-start.5
  487.4 8.7 collective-permute-done.6
  505.9 8.7 collective-permute-done.6
  524.5 8.7 collective-permute-done.6
  543.0 8.7 collective-permute-done.6
  561.5 8.7 collective-permute-done.6
  580.1 8.7 collective-permute-done.6
  598.6 8.7 collective-permute-done.6
  617.1 8.7 collective-permute-done.6
  635.7 8.7 collective-permute-done.6
  654.2 8.7 collective-permute-done.6
  664.3 4.5 collective-permute-start.5
  672.7 8.7 collective-permute-done.6
  691.3 8.7 collective-permute-done.6
  709.8 8.7 collective-permute-done.6
  728.4 8.7 collective-permute-done.6
  746.9 8.7 collective-permute-done.6
  765.4 8.7 collective-permute-done.6
  784.0 8.7 collective-permute-done.6
  802.5 8.7 collective-permute-done.6
  821.0 8.7 collective-permute-done.6
  839.6 8.7 collective-permute-done.6
  858.1 8.7 collective-permute-done.6
  (1162 shorter events, 507.5 us)
Async XLA Ops:
  122.0 25.3 %collective-permute-start.7 = (f32[1,2,32,1024]{3,2,1,0:T(8,128)S(1)}, f32[1,2,32,1024]{3,2,1,0:T(8,128)S(1)}, u32[]{:S(2)}, u32[]{:S(2)}) collective-permute-start(f32[1,2,32,1024]{3,2,1,0:T(8,128)S(1)} %get-tuple-element.162), channel_id=1, source_target_pairs={{0,4},{4,8},{8,12},{12,16},{16,20},{20,24},{24,28},{28,32},{32,36}... | collective-permute-start | bytes 786440 | tf_op jit(solution)/shard_map/ppermute | solution.py:29
  155.7 6.0 collective-permute-start.2
  285.3 27.2 %collective-permute-start.6 = (f32[1,2,32,1024]{3,2,1,0:T(8,128)S(1)}, f32[1,2,32,1024]{3,2,1,0:T(8,128)S(1)}, u32[]{:S(2)}, u32[]{:S(2)}) collective-permute-start(f32[1,2,32,1024]{3,2,1,0:T(8,128)S(1)} %multiply_add_fusion.3), channel_id=1, source_target_pairs={{0,4},{4,8},{8,12},{12,16},{16,20},{20,24},{24,28},{28,32},{32,36}... | collective-permute-start | bytes 786440 | tf_op jit(solution)/shard_map/while/body/eval_jaxpr/ppermute | solution.py:29
  312.6 5.9 collective-permute-start.4
  320.4 8.9 %collective-permute-start.6 = (f32[1,2,32,1024]{3,2,1,0:T(8,128)S(1)}, f32[1,2,32,1024]{3,2,1,0:T(8,128)S(1)}, u32[]{:S(2)}, u32[]{:S(2)}) collective-permute-start(f32[1,2,32,1024]{3,2,1,0:T(8,128)S(1)} %multiply_add_fusion.3), channel_id=1, source_target_pairs={{0,4},{4,8},{8,12},{12,16},{16,20},{20,24},{24,28},{28,32},{32,36}... | collective-permute-start | bytes 786440 | tf_op jit(solution)/shard_map/while/body/eval_jaxpr/ppermute | solution.py:29
  337.2 10.7 %collective-permute-start.6 = (f32[1,2,32,1024]{3,2,1,0:T(8,128)S(1)}, f32[1,2,32,1024]{3,2,1,0:T(8,128)S(1)}, u32[]{:S(2)}, u32[]{:S(2)}) collective-permute-start(f32[1,2,32,1024]{3,2,1,0:T(8,128)S(1)} %multiply_add_fusion.3), channel_id=1, source_target_pairs={{0,4},{4,8},{8,12},{12,16},{16,20},{20,24},{24,28},{28,32},{32,36}... | collective-permute-start | bytes 786440 | tf_op jit(solution)/shard_map/while/body/eval_jaxpr/ppermute | solution.py:29
  355.7 10.7 %collective-permute-start.6 = (f32[1,2,32,1024]{3,2,1,0:T(8,128)S(1)}, f32[1,2,32,1024]{3,2,1,0:T(8,128)S(1)}, u32[]{:S(2)}, u32[]{:S(2)}) collective-permute-start(f32[1,2,32,1024]{3,2,1,0:T(8,128)S(1)} %multiply_add_fusion.3), channel_id=1, source_target_pairs={{0,4},{4,8},{8,12},{12,16},{16,20},{20,24},{24,28},{28,32},{32,36}... | collective-permute-start | bytes 786440 | tf_op jit(solution)/shard_map/while/body/eval_jaxpr/ppermute | solution.py:29
  366.5 5.9 collective-permute-start.4
  374.3 10.7 %collective-permute-start.6 = (f32[1,2,32,1024]{3,2,1,0:T(8,128)S(1)}, f32[1,2,32,1024]{3,2,1,0:T(8,128)S(1)}, u32[]{:S(2)}, u32[]{:S(2)}) collective-permute-start(f32[1,2,32,1024]{3,2,1,0:T(8,128)S(1)} %multiply_add_fusion.3), channel_id=1, source_target_pairs={{0,4},{4,8},{8,12},{12,16},{16,20},{20,24},{24,28},{28,32},{32,36}... | collective-permute-start | bytes 786440 | tf_op jit(solution)/shard_map/while/body/eval_jaxpr/ppermute | solution.py:29
  385.0 5.9 collective-permute-start.4
  392.8 10.7 %collective-permute-start.6 = (f32[1,2,32,1024]{3,2,1,0:T(8,128)S(1)}, f32[1,2,32,1024]{3,2,1,0:T(8,128)S(1)}, u32[]{:S(2)}, u32[]{:S(2)}) collective-permute-start(f32[1,2,32,1024]{3,2,1,0:T(8,128)S(1)} %multiply_add_fusion.3), channel_id=1, source_target_pairs={{0,4},{4,8},{8,12},{12,16},{16,20},{20,24},{24,28},{28,32},{32,36}... | collective-permute-start | bytes 786440 | tf_op jit(solution)/shard_map/while/body/eval_jaxpr/ppermute | solution.py:29
  403.5 5.9 collective-permute-start.4
  411.3 10.7 %collective-permute-start.6 = (f32[1,2,32,1024]{3,2,1,0:T(8,128)S(1)}, f32[1,2,32,1024]{3,2,1,0:T(8,128)S(1)}, u32[]{:S(2)}, u32[]{:S(2)}) collective-permute-start(f32[1,2,32,1024]{3,2,1,0:T(8,128)S(1)} %multiply_add_fusion.3), channel_id=1, source_target_pairs={{0,4},{4,8},{8,12},{12,16},{16,20},{20,24},{24,28},{28,32},{32,36}... | collective-permute-start | bytes 786440 | tf_op jit(solution)/shard_map/while/body/eval_jaxpr/ppermute | solution.py:29
  422.1 5.9 collective-permute-start.4
  429.9 10.7 %collective-permute-start.6 = (f32[1,2,32,1024]{3,2,1,0:T(8,128)S(1)}, f32[1,2,32,1024]{3,2,1,0:T(8,128)S(1)}, u32[]{:S(2)}, u32[]{:S(2)}) collective-permute-start(f32[1,2,32,1024]{3,2,1,0:T(8,128)S(1)} %multiply_add_fusion.3), channel_id=1, source_target_pairs={{0,4},{4,8},{8,12},{12,16},{16,20},{20,24},{24,28},{28,32},{32,36}... | collective-permute-start | bytes 786440 | tf_op jit(solution)/shard_map/while/body/eval_jaxpr/ppermute | solution.py:29
  448.4 10.7 %collective-permute-start.6 = (f32[1,2,32,1024]{3,2,1,0:T(8,128)S(1)}, f32[1,2,32,1024]{3,2,1,0:T(8,128)S(1)}, u32[]{:S(2)}, u32[]{:S(2)}) collective-permute-start(f32[1,2,32,1024]{3,2,1,0:T(8,128)S(1)} %multiply_add_fusion.3), channel_id=1, source_target_pairs={{0,4},{4,8},{8,12},{12,16},{16,20},{20,24},{24,28},{28,32},{32,36}... | collective-permute-start | bytes 786440 | tf_op jit(solution)/shard_map/while/body/eval_jaxpr/ppermute | solution.py:29
  466.9 10.7 %collective-permute-start.6 = (f32[1,2,32,1024]{3,2,1,0:T(8,128)S(1)}, f32[1,2,32,1024]{3,2,1,0:T(8,128)S(1)}, u32[]{:S(2)}, u32[]{:S(2)}) collective-permute-start(f32[1,2,32,1024]{3,2,1,0:T(8,128)S(1)} %multiply_add_fusion.3), channel_id=1, source_target_pairs={{0,4},{4,8},{8,12},{12,16},{16,20},{20,24},{24,28},{28,32},{32,36}... | collective-permute-start | bytes 786440 | tf_op jit(solution)/shard_map/while/body/eval_jaxpr/ppermute | solution.py:29
  477.7 5.9 collective-permute-start.4
  485.5 10.7 %collective-permute-start.6 = (f32[1,2,32,1024]{3,2,1,0:T(8,128)S(1)}, f32[1,2,32,1024]{3,2,1,0:T(8,128)S(1)}, u32[]{:S(2)}, u32[]{:S(2)}) collective-permute-start(f32[1,2,32,1024]{3,2,1,0:T(8,128)S(1)} %multiply_add_fusion.3), channel_id=1, source_target_pairs={{0,4},{4,8},{8,12},{12,16},{16,20},{20,24},{24,28},{28,32},{32,36}... | collective-permute-start | bytes 786440 | tf_op jit(solution)/shard_map/while/body/eval_jaxpr/ppermute | solution.py:29
  496.2 5.9 collective-permute-start.4
  504.0 10.7 %collective-permute-start.6 = (f32[1,2,32,1024]{3,2,1,0:T(8,128)S(1)}, f32[1,2,32,1024]{3,2,1,0:T(8,128)S(1)}, u32[]{:S(2)}, u32[]{:S(2)}) collective-permute-start(f32[1,2,32,1024]{3,2,1,0:T(8,128)S(1)} %multiply_add_fusion.3), channel_id=1, source_target_pairs={{0,4},{4,8},{8,12},{12,16},{16,20},{20,24},{24,28},{28,32},{32,36}... | collective-permute-start | bytes 786440 | tf_op jit(solution)/shard_map/while/body/eval_jaxpr/ppermute | solution.py:29
  514.8 5.9 collective-permute-start.4
  522.5 10.7 %collective-permute-start.6 = (f32[1,2,32,1024]{3,2,1,0:T(8,128)S(1)}, f32[1,2,32,1024]{3,2,1,0:T(8,128)S(1)}, u32[]{:S(2)}, u32[]{:S(2)}) collective-permute-start(f32[1,2,32,1024]{3,2,1,0:T(8,128)S(1)} %multiply_add_fusion.3), channel_id=1, source_target_pairs={{0,4},{4,8},{8,12},{12,16},{16,20},{20,24},{24,28},{28,32},{32,36}... | collective-permute-start | bytes 786440 | tf_op jit(solution)/shard_map/while/body/eval_jaxpr/ppermute | solution.py:29
  533.3 5.9 collective-permute-start.4
  541.1 10.7 %collective-permute-start.6 = (f32[1,2,32,1024]{3,2,1,0:T(8,128)S(1)}, f32[1,2,32,1024]{3,2,1,0:T(8,128)S(1)}, u32[]{:S(2)}, u32[]{:S(2)}) collective-permute-start(f32[1,2,32,1024]{3,2,1,0:T(8,128)S(1)} %multiply_add_fusion.3), channel_id=1, source_target_pairs={{0,4},{4,8},{8,12},{12,16},{16,20},{20,24},{24,28},{28,32},{32,36}... | collective-permute-start | bytes 786440 | tf_op jit(solution)/shard_map/while/body/eval_jaxpr/ppermute | solution.py:29
  559.6 10.7 %collective-permute-start.6 = (f32[1,2,32,1024]{3,2,1,0:T(8,128)S(1)}, f32[1,2,32,1024]{3,2,1,0:T(8,128)S(1)}, u32[]{:S(2)}, u32[]{:S(2)}) collective-permute-start(f32[1,2,32,1024]{3,2,1,0:T(8,128)S(1)} %multiply_add_fusion.3), channel_id=1, source_target_pairs={{0,4},{4,8},{8,12},{12,16},{16,20},{20,24},{24,28},{28,32},{32,36}... | collective-permute-start | bytes 786440 | tf_op jit(solution)/shard_map/while/body/eval_jaxpr/ppermute | solution.py:29
  578.1 10.7 %collective-permute-start.6 = (f32[1,2,32,1024]{3,2,1,0:T(8,128)S(1)}, f32[1,2,32,1024]{3,2,1,0:T(8,128)S(1)}, u32[]{:S(2)}, u32[]{:S(2)}) collective-permute-start(f32[1,2,32,1024]{3,2,1,0:T(8,128)S(1)} %multiply_add_fusion.3), channel_id=1, source_target_pairs={{0,4},{4,8},{8,12},{12,16},{16,20},{20,24},{24,28},{28,32},{32,36}... | collective-permute-start | bytes 786440 | tf_op jit(solution)/shard_map/while/body/eval_jaxpr/ppermute | solution.py:29
  596.7 10.7 %collective-permute-start.6 = (f32[1,2,32,1024]{3,2,1,0:T(8,128)S(1)}, f32[1,2,32,1024]{3,2,1,0:T(8,128)S(1)}, u32[]{:S(2)}, u32[]{:S(2)}) collective-permute-start(f32[1,2,32,1024]{3,2,1,0:T(8,128)S(1)} %multiply_add_fusion.3), channel_id=1, source_target_pairs={{0,4},{4,8},{8,12},{12,16},{16,20},{20,24},{24,28},{28,32},{32,36}... | collective-permute-start | bytes 786440 | tf_op jit(solution)/shard_map/while/body/eval_jaxpr/ppermute | solution.py:29
  607.4 5.9 collective-permute-start.4
  615.2 10.7 %collective-permute-start.6 = (f32[1,2,32,1024]{3,2,1,0:T(8,128)S(1)}, f32[1,2,32,1024]{3,2,1,0:T(8,128)S(1)}, u32[]{:S(2)}, u32[]{:S(2)}) collective-permute-start(f32[1,2,32,1024]{3,2,1,0:T(8,128)S(1)} %multiply_add_fusion.3), channel_id=1, source_target_pairs={{0,4},{4,8},{8,12},{12,16},{16,20},{20,24},{24,28},{28,32},{32,36}... | collective-permute-start | bytes 786440 | tf_op jit(solution)/shard_map/while/body/eval_jaxpr/ppermute | solution.py:29
  626.0 5.9 collective-permute-start.4
  633.8 10.7 %collective-permute-start.6 = (f32[1,2,32,1024]{3,2,1,0:T(8,128)S(1)}, f32[1,2,32,1024]{3,2,1,0:T(8,128)S(1)}, u32[]{:S(2)}, u32[]{:S(2)}) collective-permute-start(f32[1,2,32,1024]{3,2,1,0:T(8,128)S(1)} %multiply_add_fusion.3), channel_id=1, source_target_pairs={{0,4},{4,8},{8,12},{12,16},{16,20},{20,24},{24,28},{28,32},{32,36}... | collective-permute-start | bytes 786440 | tf_op jit(solution)/shard_map/while/body/eval_jaxpr/ppermute | solution.py:29
  644.5 5.9 collective-permute-start.4
  652.3 10.7 %collective-permute-start.6 = (f32[1,2,32,1024]{3,2,1,0:T(8,128)S(1)}, f32[1,2,32,1024]{3,2,1,0:T(8,128)S(1)}, u32[]{:S(2)}, u32[]{:S(2)}) collective-permute-start(f32[1,2,32,1024]{3,2,1,0:T(8,128)S(1)} %multiply_add_fusion.3), channel_id=1, source_target_pairs={{0,4},{4,8},{8,12},{12,16},{16,20},{20,24},{24,28},{28,32},{32,36}... | collective-permute-start | bytes 786440 | tf_op jit(solution)/shard_map/while/body/eval_jaxpr/ppermute | solution.py:29
  663.0 5.9 collective-permute-start.4
  670.8 10.7 %collective-permute-start.6 = (f32[1,2,32,1024]{3,2,1,0:T(8,128)S(1)}, f32[1,2,32,1024]{3,2,1,0:T(8,128)S(1)}, u32[]{:S(2)}, u32[]{:S(2)}) collective-permute-start(f32[1,2,32,1024]{3,2,1,0:T(8,128)S(1)} %multiply_add_fusion.3), channel_id=1, source_target_pairs={{0,4},{4,8},{8,12},{12,16},{16,20},{20,24},{24,28},{28,32},{32,36}... | collective-permute-start | bytes 786440 | tf_op jit(solution)/shard_map/while/body/eval_jaxpr/ppermute | solution.py:29
  689.4 10.7 %collective-permute-start.6 = (f32[1,2,32,1024]{3,2,1,0:T(8,128)S(1)}, f32[1,2,32,1024]{3,2,1,0:T(8,128)S(1)}, u32[]{:S(2)}, u32[]{:S(2)}) collective-permute-start(f32[1,2,32,1024]{3,2,1,0:T(8,128)S(1)} %multiply_add_fusion.3), channel_id=1, source_target_pairs={{0,4},{4,8},{8,12},{12,16},{16,20},{20,24},{24,28},{28,32},{32,36}... | collective-permute-start | bytes 786440 | tf_op jit(solution)/shard_map/while/body/eval_jaxpr/ppermute | solution.py:29
  707.9 10.7 %collective-permute-start.6 = (f32[1,2,32,1024]{3,2,1,0:T(8,128)S(1)}, f32[1,2,32,1024]{3,2,1,0:T(8,128)S(1)}, u32[]{:S(2)}, u32[]{:S(2)}) collective-permute-start(f32[1,2,32,1024]{3,2,1,0:T(8,128)S(1)} %multiply_add_fusion.3), channel_id=1, source_target_pairs={{0,4},{4,8},{8,12},{12,16},{16,20},{20,24},{24,28},{28,32},{32,36}... | collective-permute-start | bytes 786440 | tf_op jit(solution)/shard_map/while/body/eval_jaxpr/ppermute | solution.py:29
  718.6 5.9 collective-permute-start.4
  726.4 10.7 %collective-permute-start.6 = (f32[1,2,32,1024]{3,2,1,0:T(8,128)S(1)}, f32[1,2,32,1024]{3,2,1,0:T(8,128)S(1)}, u32[]{:S(2)}, u32[]{:S(2)}) collective-permute-start(f32[1,2,32,1024]{3,2,1,0:T(8,128)S(1)} %multiply_add_fusion.3), channel_id=1, source_target_pairs={{0,4},{4,8},{8,12},{12,16},{16,20},{20,24},{24,28},{28,32},{32,36}... | collective-permute-start | bytes 786440 | tf_op jit(solution)/shard_map/while/body/eval_jaxpr/ppermute | solution.py:29
  737.2 5.9 collective-permute-start.4
  745.0 10.7 %collective-permute-start.6 = (f32[1,2,32,1024]{3,2,1,0:T(8,128)S(1)}, f32[1,2,32,1024]{3,2,1,0:T(8,128)S(1)}, u32[]{:S(2)}, u32[]{:S(2)}) collective-permute-start(f32[1,2,32,1024]{3,2,1,0:T(8,128)S(1)} %multiply_add_fusion.3), channel_id=1, source_target_pairs={{0,4},{4,8},{8,12},{12,16},{16,20},{20,24},{24,28},{28,32},{32,36}... | collective-permute-start | bytes 786440 | tf_op jit(solution)/shard_map/while/body/eval_jaxpr/ppermute | solution.py:29
  763.5 10.7 %collective-permute-start.6 = (f32[1,2,32,1024]{3,2,1,0:T(8,128)S(1)}, f32[1,2,32,1024]{3,2,1,0:T(8,128)S(1)}, u32[]{:S(2)}, u32[]{:S(2)}) collective-permute-start(f32[1,2,32,1024]{3,2,1,0:T(8,128)S(1)} %multiply_add_fusion.3), channel_id=1, source_target_pairs={{0,4},{4,8},{8,12},{12,16},{16,20},{20,24},{24,28},{28,32},{32,36}... | collective-permute-start | bytes 786440 | tf_op jit(solution)/shard_map/while/body/eval_jaxpr/ppermute | solution.py:29
  782.0 10.7 %collective-permute-start.6 = (f32[1,2,32,1024]{3,2,1,0:T(8,128)S(1)}, f32[1,2,32,1024]{3,2,1,0:T(8,128)S(1)}, u32[]{:S(2)}, u32[]{:S(2)}) collective-permute-start(f32[1,2,32,1024]{3,2,1,0:T(8,128)S(1)} %multiply_add_fusion.3), channel_id=1, source_target_pairs={{0,4},{4,8},{8,12},{12,16},{16,20},{20,24},{24,28},{28,32},{32,36}... | collective-permute-start | bytes 786440 | tf_op jit(solution)/shard_map/while/body/eval_jaxpr/ppermute | solution.py:29
  800.6 10.7 %collective-permute-start.6 = (f32[1,2,32,1024]{3,2,1,0:T(8,128)S(1)}, f32[1,2,32,1024]{3,2,1,0:T(8,128)S(1)}, u32[]{:S(2)}, u32[]{:S(2)}) collective-permute-start(f32[1,2,32,1024]{3,2,1,0:T(8,128)S(1)} %multiply_add_fusion.3), channel_id=1, source_target_pairs={{0,4},{4,8},{8,12},{12,16},{16,20},{20,24},{24,28},{28,32},{32,36}... | collective-permute-start | bytes 786440 | tf_op jit(solution)/shard_map/while/body/eval_jaxpr/ppermute | solution.py:29
  819.1 10.7 %collective-permute-start.6 = (f32[1,2,32,1024]{3,2,1,0:T(8,128)S(1)}, f32[1,2,32,1024]{3,2,1,0:T(8,128)S(1)}, u32[]{:S(2)}, u32[]{:S(2)}) collective-permute-start(f32[1,2,32,1024]{3,2,1,0:T(8,128)S(1)} %multiply_add_fusion.3), channel_id=1, source_target_pairs={{0,4},{4,8},{8,12},{12,16},{16,20},{20,24},{24,28},{28,32},{32,36}... | collective-permute-start | bytes 786440 | tf_op jit(solution)/shard_map/while/body/eval_jaxpr/ppermute | solution.py:29
  837.6 10.7 %collective-permute-start.6 = (f32[1,2,32,1024]{3,2,1,0:T(8,128)S(1)}, f32[1,2,32,1024]{3,2,1,0:T(8,128)S(1)}, u32[]{:S(2)}, u32[]{:S(2)}) collective-permute-start(f32[1,2,32,1024]{3,2,1,0:T(8,128)S(1)} %multiply_add_fusion.3), channel_id=1, source_target_pairs={{0,4},{4,8},{8,12},{12,16},{16,20},{20,24},{24,28},{28,32},{32,36}... | collective-permute-start | bytes 786440 | tf_op jit(solution)/shard_map/while/body/eval_jaxpr/ppermute | solution.py:29
  856.2 10.7 %collective-permute-start.6 = (f32[1,2,32,1024]{3,2,1,0:T(8,128)S(1)}, f32[1,2,32,1024]{3,2,1,0:T(8,128)S(1)}, u32[]{:S(2)}, u32[]{:S(2)}) collective-permute-start(f32[1,2,32,1024]{3,2,1,0:T(8,128)S(1)} %multiply_add_fusion.3), channel_id=1, source_target_pairs={{0,4},{4,8},{8,12},{12,16},{16,20},{20,24},{24,28},{28,32},{32,36}... | collective-permute-start | bytes 786440 | tf_op jit(solution)/shard_map/while/body/eval_jaxpr/ppermute | solution.py:29
  (119 other events, 899.7 us)
where the time goes:
time: 889 us; the launch traced here: 875 us
  starting transfers between devices  482 us (54%)
  waiting for transfers between devices  311 us (35%)
  other arithmetic  46.1 us (5%)
  local copies, waits for them, and re-layouts  28.3 us (3%)
    ppermute x65, starting transfers between devices, padded_2(): before = lax.ppermute(last, axis, up)  287 us
    ppermute x32, waiting for transfers between devices, passed_along(): return lax.ppermute(shard, axis, pairs)  260 us
    ppermute x32, starting transfers between devices, passed_along(): return lax.ppermute(shard, axis, pairs)  111 us
    ppermute x65, starting transfers between devices, padded_2(): after = lax.ppermute(initial, axis, down)  84.3 us
    ppermute x65, waiting for transfers between devices, padded_2(): before = lax.ppermute(last, axis, up)  51.3 us
    mul x65, other arithmetic, heun_padded(): middle = middle * section_mask(first_row + 1, middle.shape[-2], total_rows)  18.7 us
  transfers between devices with their start and end apart: 162, of which 97 were waited for; matrix products, arithmetic and copies ran while one was open for 0% of the time, Pallas kernels for 0%

commit v1 on v0

v1 whole, which is shorter than its diff:
```python
import jax
import jax.numpy as jnp
from jax import lax
from jax.experimental import pallas as pl
from jax.experimental.pallas import tpu as pltpu
from jax.sharding import PartitionSpec as P

MESH = pl.DeviceIdType.MESH
F32 = jnp.float32
H = 0.015625
SCALE = H / 2
VISC = 0.8
FINE = (1.0 - 4.0 * VISC * H, VISC * H, 1.0)
COARSE = (1.0 - 64.0 * VISC * H, 16.0 * VISC * H, 16.0)
WINDOW = 384
OFF = 8
ROWS = 432
B = 32
HALO = 64
GW = B + 2 * HALO


def stage(src, o, masks, consts):
    c0, k, q = consts
    u = src[0, pl.ds(o, 8), :]
    v = src[1, pl.ds(o, 8), :]
    su, sv = (u, v) if q == 1.0 else (q * u, q * v)
    a, b = k - su, k + su
    c = jnp.where(masks[0], k - sv, 0.0)
    d = jnp.where(masks[1], k + sv, 0.0)
    out = []
    for i, x in ((0, u), (1, v)):
        east = src[i, pl.ds(o + 1, 8), :]
        west = src[i, pl.ds(o - 1, 8), :]
        north = pltpu.roll(x, 127, 1)
        south = pltpu.roll(x, 1, 1)
        out.append((c0 * x + a * east) + (b * west + c * north) + d * south)
    return out


def heun(src, mid, dst, start, n1, n2, masks, consts, dst_shift=0, extra=None):
    for i in range(n1):
        o = start - 1 + 8 * i
        m = stage(src, o, masks, consts)
        for c in range(2):
            mid[c, pl.ds(o, 8), :] = m[c]
    for i in range(n2):
        o = start + 8 * i
        m = stage(mid, o, masks, consts)
        for c in range(2):
            new = 0.5 * (src[c, pl.ds(o, 8), :] + m[c])
            if extra is not None:
                new = new + extra(c, o)
            dst[c, pl.ds(o + dst_shift, 8), :] = new


def fine_steps(first, count, even, odd, mid, masks):
    for g in range(first, first + count, 8):
        n1 = (WINDOW - 2 - 4 * g + 7) // 8
        n2 = (WINDOW - 4 - 4 * g + 7) // 8

        def body(t, _):
            for p, (src, dst) in enumerate(((even, odd), (odd, even))):
                start = OFF + 2 * (2 * t + p) + 2
                heun(src, mid, dst, start, n1, n2, masks, FINE)
            return 0

        lax.fori_loop(g // 2, g // 2 + 4, body, 0)


def halo_of(j):
    return 16 * ((30 - j + 7) // 8)


CLASSES = ((0, 6, 64), (6, 14, 48), (14, 22, 32), (22, 30, 16), (30, 31, 0))


def worker_tm(r):
    y = r // 2
    return y * 8 + (2 * (r % 2) + y % 2) * 2


def kernel(
    x_ref, coarse_ref, resid_ref,
    rot, win, abuf, bbuf, dbuf, mid, cbuf, terms, relin, got, s0, s1, smid, ret, back, nres,
    xs, xr, ysem, rels, relr, gs, gr, rets, retr, ress, resr, row0s, row0r,
):
    j = lax.axis_index("tm")
    s = lax.axis_index("space")
    y, q = j // 8, lax.rem(j, 8)
    lane = lax.broadcasted_iota(jnp.int32, (8, 128), 1)
    masks = (lane < 127, lane > 0)

    low = lax.broadcasted_iota(jnp.int32, (32, 128), 1) < 64
    for c in range(2):
        turned = [pltpu.roll(x_ref[0, c, :, 128 * t : 128 * t + 128], 64, 1) for t in range(8)]
        for t in range(9):
            rot[c, :, 128 * t : 128 * t + 128] = jnp.where(low, turned[(t - 1) % 8], turned[t % 8])

    barrier = pltpu.get_barrier_semaphore()
    ring_x = [(j, lax.rem(s + d, 4)) for d in (1, 2, 3)]
    ring_y = [(lax.rem(y + d, 4) * 8 + q, s) for d in (1, 2, 3)]
    plane = [(y * 8 + lax.rem(q + d, 8), s) for d in range(1, 8)]
    for other in ring_x + ring_y + plane:
        pl.semaphore_signal(barrier, inc=1, device_id=other, device_id_type=MESH)
    pl.semaphore_wait(barrier, 13)

    sends = []
    for d in (1, 2, 3):
        to = lax.rem(s + d, 4)
        cp = pltpu.make_async_remote_copy(
            src_ref=rot.at[:, :, pl.ds(pl.multiple_of(256 * to, 128), WINDOW)],
            dst_ref=win.at[s],
            send_sem=xs.at[d - 1],
            recv_sem=xr.at[d - 1],
            device_id=(j, to),
            device_id_type=MESH,
        )
        cp.start()
        sends.append(cp)
    win[s] = rot[:, :, pl.ds(pl.multiple_of(256 * s, 128), WINDOW)]
    for cp in sends:
        cp.wait()
    for other in ring_y:
        pl.semaphore_signal(ysem, inc=1, device_id=other, device_id_type=MESH)
    for c in range(2):
        for t in range(3):
            tile = jnp.concatenate([win[i, c, :, 128 * t : 128 * t + 128] for i in range(4)], axis=0)
            abuf[c, OFF + 128 * t : OFF + 128 * t + 128, :] = tile.T * SCALE

    fine_steps(0, 16, abuf, bbuf, mid, masks)

    pl.semaphore_wait(ysem, 3)
    own = pl.ds(OFF + 64, 256)
    before = pltpu.make_async_remote_copy(
        src_ref=abuf.at[:, own, :], dst_ref=relin, send_sem=rels, recv_sem=relr,
        device_id=(lax.rem(j + 31, 32), s), device_id_type=MESH,
    )
    before.start()

    heun(abuf, mid, cbuf, OFF + 64, 33, 32, masks, COARSE, dst_shift=-(OFF + 64))
    for c in range(2):
        dbuf[c, :, :] = abuf[c, :, :]
    fine_steps(16, 16, dbuf, bbuf, mid, masks)

    for i in range(32):
        for c in range(2):
            rows = pl.ds(8 * i, 8)
            coarse = jnp.where(j > 0, cbuf[c, rows, :], 0.0)
            terms[c, rows, :] = dbuf[c, pl.ds(OFF + 64 + 8 * i, 8), :] - coarse

    def gather(act):
        for first, last, h in CLASSES:

            def pieces(h=h):
                for r in range(-2, 10):
                    lo, hi = max(0, B * r - h), min(256, B * r + B + h)
                    if hi <= lo:
                        continue
                    at = lo - (B * r - HALO)
                    src = terms.at[:, pl.ds(lo, hi - lo), :]
                    dst = got.at[j, :, pl.ds(at, hi - lo), :]
                    holder = worker_tm(r % 8)
                    to = lax.rem(s + (r // 8) + 4, 4)

                    def remote(src=src, dst=dst, r=r, holder=holder, to=to):
                        act(
                            pltpu.make_async_remote_copy(
                                src_ref=src, dst_ref=dst, send_sem=gs.at[r + 2], recv_sem=gr.at[j],
                                device_id=(holder, to), device_id_type=MESH,
                            ),
                            True,
                        )

                    if 0 <= r < 8:
                        pl.when(j != holder)(remote)

                        @pl.when(j == holder)
                        def _(src=src, dst=dst):
                            act(pltpu.make_async_copy(src, dst, gr.at[j]), False)
                    else:
                        remote()

            pl.when((j >= first) & (j < last))(pieces)

    def start(copy, remote):
        copy.start()

    gather(start)

    before.wait()

    @pl.when(j < 31)
    def _():
        for c in range(2):
            for t in range(2):
                rows = pl.ds(OFF + 64 + 128 * t, 128)
                diff = (dbuf[c, rows, :] - relin[c, 128 * t : 128 * t + 128, :]) * (1.0 / SCALE)
                diff = diff.T
                for i in range(4):
                    nres[i, c, :, 128 * t : 128 * t + 128] = diff[32 * i : 32 * i + 32, :]

    @pl.when(j == 31)
    def _():
        for c in range(2):
            for t in range(2):
                for i in range(4):
                    nres[i, c, :, 128 * t : 128 * t + 128] = jnp.zeros((32, 128), F32)

    columns = pl.ds(pl.multiple_of(256 * s, 128), 256)
    res_copies = []
    for i in range(4):
        cp = pltpu.make_async_remote_copy(
            src_ref=nres.at[i], dst_ref=resid_ref.at[0, :, :, columns], send_sem=ress.at[i], recv_sem=resr,
            device_id=(lax.rem(j + 1, 32), i), device_id_type=MESH,
        )
        cp.start()
        res_copies.append(cp)

    r_me = 2 * y + lax.rem(q // 2, 4) // 2
    is_worker = q == 4 * lax.rem(r_me, 2) + 2 * lax.rem(y, 2)
    block = 8 * s + r_me
    group = lane // 32

    def send_back(j_at, state, base):
        for c in range(2):
            parts = [state(c, base + 8 * g) for g in range(4)]
            for i in range(4):
                acc = pltpu.roll(parts[0], (128 - 32 * i) % 128, 1) if i else parts[0]
                for g in range(1, 4):
                    amount = (32 * (g - i)) % 128
                    part = pltpu.roll(parts[g], amount, 1) if amount else parts[g]
                    acc = jnp.where(group == g, part, acc)
                ret[4 * j_at + i, c, :, :] = acc
        for i in range(4):
            mine = (j_at + 1 == j) & (s == i)

            @pl.when(jnp.logical_not(mine))
            def _(i=i):
                pltpu.make_async_remote_copy(
                    src_ref=ret.at[4 * j_at + i], dst_ref=back.at[block], send_sem=rets, recv_sem=retr,
                    device_id=(j_at + 1, i), device_id_type=MESH,
                ).start()

            @pl.when(mine)
            def _(i=i):
                pltpu.make_async_copy(ret.at[4 * j_at + i], back.at[block], retr).start()

    def await_terms(j_at, h):
        view = got.at[j_at, :, pl.ds(HALO - h, B + 2 * h), :]
        pltpu.make_async_copy(view, view, gr.at[j_at]).wait()

    @pl.when(is_worker)
    def _():
        await_terms(0, 64)
        for c in range(2):
            s0[c, pl.ds(OFF, GW), :] = got[0, c, :GW, :]
        send_back(0, lambda c, o: s0[c, pl.ds(o, 8), :], OFF + HALO)

        def pair(j_first, h_first, h_second, n1, n2):
            for p, (src, dst, h) in enumerate(((s0, s1, h_first), (s1, s0, h_second))):
                at = j_first + p
                await_terms(at, h)
                begin = OFF + HALO - 2 * (30 - at)
                heun(
                    src, smid, dst, begin, n1, n2, masks, COARSE,
                    extra=lambda c, o, at=at: got[at, c, pl.ds(o - OFF, 8), :],
                )
                send_back(at, lambda c, o, dst=dst: dst[c, pl.ds(o, 8), :], OFF + HALO)

        at = 1
        while at < 30:
            h1, h2 = halo_of(at), halo_of(at + 1)
            end = at + 2
            while end < 30 and (halo_of(end), halo_of(end + 1)) == (h1, h2) and end - at < 4:
                end += 2
            width = B + 4 * (30 - at)
            n1, n2 = (width + 2 + 7) // 8, (width + 7) // 8
            if end - at > 2:

                def body(t, _, at=at, h1=h1, h2=h2, n1=n1, n2=n2):
                    pair(at + 2 * t, h1, h2, n1, n2)
                    return 0

                lax.fori_loop(0, (end - at) // 2, body, 0)
            else:
                pair(at, h1, h2, n1, n2)
            at = end

    @pl.when(j == 0)
    def _():
        for c in range(2):
            for t in range(2):
                turned = (abuf[c, pl.ds(OFF + 64 + 128 * t, 128), :] * (1.0 / SCALE)).T
                for i in range(4):
                    win[i, c, :, 128 * t : 128 * t + 128] = turned[32 * i : 32 * i + 32, :]
        coarse_ref[0, :, :, columns] = win[s, :, :, :256]
        copies = []
        for d in (1, 2, 3):
            to = lax.rem(s + d, 4)
            cp = pltpu.make_async_remote_copy(
                src_ref=win.at[to, :, :, pl.ds(0, 256)], dst_ref=coarse_ref.at[0, :, :, columns],
                send_sem=row0s.at[d - 1], recv_sem=row0r.at[d - 1], device_id=(j, to), device_id_type=MESH,
            )
            cp.start()
            copies.append(cp)
        for cp in copies:
            cp.wait()

    @pl.when(j > 0)
    def _():
        pltpu.make_async_copy(back, back, retr).wait()
        for c in range(2):
            for half in range(2):
                strips = []
                for e in range(4):
                    packed = [back[16 * half + 4 * k + e, c, :, :] for k in range(4)]
                    for g in range(4):
                        acc = None
                        for k in range(4):
                            amount = (32 * (k - g)) % 128
                            part = pltpu.roll(packed[k], amount, 1) if amount else packed[k]
                            acc = part if acc is None else jnp.where(group == k, part, acc)
                        strips.append(acc)
                square = (jnp.concatenate(strips, axis=0) * (1.0 / SCALE)).T
                for k in range(4):
                    tile = 4 * half + k
                    coarse_ref[0, c, :, 128 * tile : 128 * tile + 128] = square[32 * k : 32 * k + 32, :]

    pltpu.make_async_copy(resid_ref, resid_ref, resr).wait()
    for cp in res_copies:
        cp.wait_send()

    def finish(copy, remote):
        if remote:
            copy.wait_send()

    gather(finish)

    @pl.when(is_worker & (j > 0))
    def _():
        view = ret.at[pl.ds(0, 123)]
        pltpu.make_async_copy(view, view, rets).wait()

    @pl.when(is_worker & (j == 0))
    def _():
        pltpu.make_async_copy(ret, ret, rets).wait()


def on_device(iterate):
    vmem = pl.BlockSpec(memory_space=pltpu.VMEM)
    dma = pltpu.SemaphoreType.DMA
    shape = jax.ShapeDtypeStruct((1, 2, 32, 1024), F32)
    return pl.pallas_call(
        kernel,
        out_shape=(shape, shape),
        in_specs=[vmem],
        out_specs=(vmem, vmem),
        scratch_shapes=[
            pltpu.VMEM((2, 32, 1152), F32),
            pltpu.VMEM((4, 2, 32, WINDOW), F32),
            pltpu.VMEM((2, ROWS, 128), F32),
            pltpu.VMEM((2, ROWS, 128), F32),
            pltpu.VMEM((2, ROWS, 128), F32),
            pltpu.VMEM((2, ROWS, 128), F32),
            pltpu.VMEM((2, 256, 128), F32),
            pltpu.VMEM((2, 256, 128), F32),
            pltpu.VMEM((2, 256, 128), F32),
            pltpu.VMEM((31, 2, GW + 16, 128), F32),
            pltpu.VMEM((2, GW + 32, 128), F32),
            pltpu.VMEM((2, GW + 32, 128), F32),
            pltpu.VMEM((2, GW + 32, 128), F32),
            pltpu.VMEM((124, 2, 8, 128), F32),
            pltpu.VMEM((32, 2, 8, 128), F32),
            pltpu.VMEM((4, 2, 32, 256), F32),
            dma((3,)), dma((3,)),
            pltpu.SemaphoreType.REGULAR,
            dma, dma,
            dma((12,)), dma((31,)),
            dma, dma,
            dma((4,)), dma,
            dma((3,)), dma((3,)),
        ],
        compiler_params=pltpu.CompilerParams(
            collective_id=0, has_side_effects=True, vmem_limit_bytes=48 * 2**20
        ),
    )(iterate)


def solution(mesh):
    spec = P("tm", None, "space", None)
    return jax.shard_map(on_device, mesh=mesh, in_specs=(spec,), out_specs=(spec, spec), check_vma=False)
```

time: 889 us -> 67.9 us (0.08); the launches traced: 875 us -> 67.8 us
  starting transfers between devices: 482 us -> 0 us
  waiting for transfers between devices: 311 us -> 0 us
  Pallas kernels: 0 us -> 64.8 us
  other arithmetic: 46.1 us -> 0 us
  local copies, waits for them, and re-layouts: 28.3 us -> 2.35 us
    ppermute x162 -> x0, starting transfers between devices: 482 us -> none  [the longest x65 287 us: padded_2(): before = lax.ppermute(last, axis, up)]
    ppermute x162 -> x0, waiting for transfers between devices: 311 us -> none  [the longest x32 260 us: passed_along(): return lax.ppermute(shard, axis, pairs)]
    pallas_call x0 -> x1, Pallas kernels: none -> 64.8 us  [on_device(): pl.pallas_call(kernel, out_shape=(shape, shape), in_specs=[vmem], out_spe...]
    mul x291 -> x0, other arithmetic: 31.6 us -> none  [the longest x65 18.7 us: heun_padded(): middle = middle * section_mask(first_row + 1, middle.shape[-2], total_rows)]
    slice x260 -> x0, local copies, waits for them, and re-layouts: 24.4 us -> none  [the longest x130 13.6 us: tendency(): left_cells = jnp.roll(center, 1, axis=-1)]
  transfers between devices with their start and end apart: 162 -> 0, of which waited for: 97 -> 0; matrix products, arithmetic and copies ran while one was open for 0% -> 0% of each run, Pallas kernels for 0% -> 0%
where the time goes in v1:
time: 67.9 us; the launch traced here: 67.8 us
  Pallas kernels  64.8 us (95%)
  local copies, waits for them, and re-layouts  2.35 us (3%)
    pallas_call x1, Pallas kernels, on_device(): pl.pallas_call(kernel, out_shape=(shape, shape), in_specs=[vmem], out_spe...  64.8 us
    unnamed x4, local copies, waits for them, and re-layouts  2.35 us

profile of v1, /device:TPU:25, one launch (start us, length us, event | category | flops | bytes accessed | tf_op | source)
XLA Modules:
  0.0 67.8 jit_solution(733289992444262888)
XLA Ops:
  0.6 0.0 copy-start
  0.6 0.9 %copy-done = f32[1,2,32,1024]{3,2,1,0:T(8,128)S(1)} copy-done((f32[1,2,32,1024]{3,2,1,0:T(8,128)S(1)}, f32[1,2,32,1024]{3,2,1,0:T(8,128)}, u32[]{:S(2)}) %copy-start) | copy-done | bytes 262168
  1.6 64.8 %shard_map.30 = (f32[1,2,32,1024]{3,2,1,0:T(8,128)S(1)}, f32[1,2,32,1024]{3,2,1,0:T(8,128)S(1)}) custom-call(f32[1,2,32,1024]{3,2,1,0:T(8,128)S(1)} %copy-done), custom_call_target="tpu_custom_call" | custom-call | tf_op jit(solution)/shard_map/pallas_call | solution.py:354
  66.4 0.7 %copy.5 = f32[1,2,32,1024]{3,2,1,0:T(8,128)} copy(f32[1,2,32,1024]{3,2,1,0:T(8,128)S(1)} %get-tuple-element.4) | data formatting | bytes 524288
  67.1 0.7 %copy.6 = f32[1,2,32,1024]{3,2,1,0:T(8,128)} copy(f32[1,2,32,1024]{3,2,1,0:T(8,128)S(1)} %get-tuple-element.5) | data formatting | bytes 524288
Async XLA Ops:
  0.6 1.0 %copy-start = (f32[1,2,32,1024]{3,2,1,0:T(8,128)S(1)}, f32[1,2,32,1024]{3,2,1,0:T(8,128)}, u32[]{:S(2)}) copy-start(f32[1,2,32,1024]{3,2,1,0:T(8,128)} %x_ref.1) | copy-start | bytes 786436

commit v2 on v1

v2 whole, which is shorter than its diff:
```python
import jax
import jax.numpy as jnp
from jax import lax
from jax.experimental import pallas as pl
from jax.experimental.pallas import tpu as pltpu
from jax.sharding import PartitionSpec as P

MESH = pl.DeviceIdType.MESH
F32 = jnp.float32
H = 0.015625
SCALE = H / 2
VISC = 0.8
FINE = (1.0 - 4.0 * VISC * H, VISC * H, 1.0)
COARSE = (1.0 - 64.0 * VISC * H, 16.0 * VISC * H, 16.0)
WINDOW = 384
OFF = 8
ROWS = 432
B = 32
HALO = 32
STEPS = 15
BATCHES = (5, 10, 13, 15)
GW = B + 2 * HALO


def stage(src, o, masks, consts):
    c0, k, q = consts
    u = src[0, pl.ds(o, 8), :]
    v = src[1, pl.ds(o, 8), :]
    su, sv = (u, v) if q == 1.0 else (q * u, q * v)
    a, b = k - su, k + su
    c = jnp.where(masks[0], k - sv, 0.0)
    d = jnp.where(masks[1], k + sv, 0.0)
    out = []
    for i, x in ((0, u), (1, v)):
        east = src[i, pl.ds(o + 1, 8), :]
        west = src[i, pl.ds(o - 1, 8), :]
        north = pltpu.roll(x, 127, 1)
        south = pltpu.roll(x, 1, 1)
        out.append((c0 * x + a * east) + (b * west + c * north) + d * south)
    return out


def heun(src, mid, dst, start, n1, n2, masks, consts, dst_shift=0, extra=None):
    for i in range(n1):
        o = start - 1 + 8 * i
        m = stage(src, o, masks, consts)
        for c in range(2):
            mid[c, pl.ds(o, 8), :] = m[c]
    for i in range(n2):
        o = start + 8 * i
        m = stage(mid, o, masks, consts)
        for c in range(2):
            new = 0.5 * (src[c, pl.ds(o, 8), :] + m[c])
            if extra is not None:
                new = new + extra(c, o)
            dst[c, pl.ds(o + dst_shift, 8), :] = new


def fine_steps(first, count, even, odd, mid, masks):
    for g in range(first, first + count, 8):
        n1 = (WINDOW - 2 - 4 * g + 7) // 8
        n2 = (WINDOW - 4 - 4 * g + 7) // 8

        def body(t, _):
            for p, (src, dst) in enumerate(((even, odd), (odd, even))):
                start = OFF + 2 * (2 * t + p) + 2
                heun(src, mid, dst, start, n1, n2, masks, FINE)
            return 0

        lax.fori_loop(g // 2, g // 2 + 4, body, 0)


def halo_of(slot):
    return 8 * ((2 * (STEPS - slot) + 7) // 8)


def slot_classes():
    edges = [n for n in range(STEPS + 1) if n == 0 or halo_of(n) != halo_of(n - 1)]
    return [(n, m, halo_of(n)) for n, m in zip(edges, edges[1:] + [STEPS + 1])]


def chain_tm(half, r):
    y = r // 4 + half * (3 - 2 * (r // 4))
    z = r // 4 * (7 - 2 * r) + r
    return 8 * y + 2 * z


def kernel(
    x_ref, coarse_ref, resid_ref,
    xbuf, rot, win, abuf, bbuf, dbuf, mid, cbuf, terms, relin, got, s0, s1, smid, ret, back, nres,
    xin, xs, xr, ysem, rels, relr, gs, gr, hs, rets, retr, ress, resr, row0s, row0r,
):
    j = lax.axis_index("tm")
    s = lax.axis_index("space")
    y, q = j // 8, lax.rem(j, 8)
    lane = lax.broadcasted_iota(jnp.int32, (8, 128), 1)
    masks = (lane < 127, lane > 0)

    fetch = pltpu.make_async_copy(x_ref.at[0], xbuf, xin)
    fetch.start()
    barrier = pltpu.get_barrier_semaphore()
    ring_x = [(j, lax.rem(s + d, 4)) for d in (1, 2, 3)]
    ring_y = [(lax.rem(y + d, 4) * 8 + q, s) for d in (1, 2, 3)]
    plane = [(y * 8 + lax.rem(q + d, 8), s) for d in range(1, 8)]
    for other in ring_x + ring_y + plane:
        pl.semaphore_signal(barrier, inc=1, device_id=other, device_id_type=MESH)
    fetch.wait()

    low = lax.broadcasted_iota(jnp.int32, (32, 128), 1) < 64
    for c in range(2):
        turned = [pltpu.roll(xbuf[c, :, 128 * t : 128 * t + 128], 64, 1) for t in range(8)]
        for t in range(9):
            rot[c, :, 128 * t : 128 * t + 128] = jnp.where(low, turned[(t - 1) % 8], turned[t % 8])

    pl.semaphore_wait(barrier, 13)

    sends = []
    for d in (1, 2, 3):
        to = lax.rem(s + d, 4)
        cp = pltpu.make_async_remote_copy(
            src_ref=rot.at[:, :, pl.ds(pl.multiple_of(256 * to, 128), WINDOW)],
            dst_ref=win.at[s],
            send_sem=xs.at[d - 1],
            recv_sem=xr.at[d - 1],
            device_id=(j, to),
            device_id_type=MESH,
        )
        cp.start()
        sends.append(cp)
    win[s] = rot[:, :, pl.ds(pl.multiple_of(256 * s, 128), WINDOW)]
    for cp in sends:
        cp.wait()
    for other in ring_y:
        pl.semaphore_signal(ysem, inc=1, device_id=other, device_id_type=MESH)
    for c in range(2):
        for t in range(3):
            tile = jnp.concatenate([win[i, c, :, 128 * t : 128 * t + 128] for i in range(4)], axis=0)
            abuf[c, OFF + 128 * t : OFF + 128 * t + 128, :] = tile.T * SCALE

    fine_steps(0, 16, abuf, bbuf, mid, masks)

    pl.semaphore_wait(ysem, 3)
    own = pl.ds(OFF + 64, 256)
    before = pltpu.make_async_remote_copy(
        src_ref=abuf.at[:, own, :], dst_ref=relin, send_sem=rels, recv_sem=relr,
        device_id=(lax.rem(j + 31, 32), s), device_id_type=MESH,
    )
    before.start()

    heun(abuf, mid, cbuf, OFF + 64, 33, 32, masks, COARSE, dst_shift=-(OFF + 64))
    for c in range(2):
        dbuf[c, :, :] = abuf[c, :, :]
    fine_steps(16, 16, dbuf, bbuf, mid, masks)

    for i in range(32):
        for c in range(2):
            rows = pl.ds(8 * i, 8)
            coarse = jnp.where(j > 0, cbuf[c, rows, :], 0.0)
            terms[c, rows, :] = dbuf[c, pl.ds(OFF + 64 + 8 * i, 8), :] - coarse

    half = j // 16
    slot = j - STEPS * half

    def gather(act):
        for first, end, h in slot_classes():

            def pieces(h=h):
                for r in range(-1, 9):
                    lo, hi = max(0, B * r - h), min(256, B * r + B + h)
                    if hi <= lo:
                        continue
                    src = terms.at[:, pl.ds(lo, hi - lo), :]
                    dst = got.at[slot, :, pl.ds(lo - (B * r - HALO), hi - lo), :]
                    holder = chain_tm(half, r % 8)
                    to = lax.rem(s + (r // 8) + 4, 4)

                    def remote(src=src, dst=dst, r=r, holder=holder, to=to):
                        act(
                            pltpu.make_async_remote_copy(
                                src_ref=src, dst_ref=dst, send_sem=gs.at[r + 1], recv_sem=gr.at[slot],
                                device_id=(holder, to), device_id_type=MESH,
                            ),
                            True,
                        )

                    if 0 <= r < 8:
                        pl.when(j != holder)(remote)

                        @pl.when(j == holder)
                        def _(src=src, dst=dst):
                            act(pltpu.make_async_copy(src, dst, gr.at[slot]), False)
                    else:
                        remote()

            pl.when((slot >= first) & (slot < end))(pieces)

    def start(copy, remote):
        copy.start()

    gather(start)

    before.wait()
    is_worker = lax.rem(j, 2) == 0
    columns = pl.ds(pl.multiple_of(256 * s, 128), 256)

    def residual():
        for c in range(2):
            for t in range(2):
                rows = pl.ds(OFF + 64 + 128 * t, 128)
                diff = dbuf[c, rows, :] - relin[c, 128 * t : 128 * t + 128, :]
                diff = jnp.where(j < 31, diff, 0.0).T
                for i in range(4):
                    nres[i, c, :, 128 * t : 128 * t + 128] = diff[32 * i : 32 * i + 32, :]
        for i in range(4):
            res_copy(i).start()

    def res_copy(i):
        return pltpu.make_async_remote_copy(
            src_ref=nres.at[i], dst_ref=resid_ref.at[0, :, :, columns], send_sem=ress.at[i], recv_sem=resr,
            device_id=(lax.rem(j + 1, 32), i), device_id_type=MESH,
        )

    def finish(copy, remote):
        if remote:
            copy.wait_send()

    @pl.when(jnp.logical_not(is_worker))
    def _():
        gather(finish)

    @pl.when(jnp.logical_not(is_worker & (half == 0)))
    def _():
        residual()

    r_me = 4 * jnp.where(half == 0, y, 3 - y) + jnp.where((y == 0) | (y == 3), q // 2, 3 - q // 2)
    block = 8 * s + r_me
    group = lane // 32

    def pack(n, state, base):
        for c in range(2):
            parts = [state[c, base + 8 * g : base + 8 * g + 8, :] for g in range(4)]
            for i in range(4):
                acc = pltpu.roll(parts[0], (128 - 32 * i) % 128, 1) if i else parts[0]
                for g in range(1, 4):
                    amount = (32 * (g - i)) % 128
                    part = pltpu.roll(parts[g], amount, 1) if amount else parts[g]
                    acc = jnp.where(group == g, part, acc)
                ret[4 * n + i, c, :, :] = acc

    def send_back(n):
        row = STEPS * half + n + 1

        def remote(i):
            pltpu.make_async_remote_copy(
                src_ref=ret.at[4 * n + i], dst_ref=back.at[block], send_sem=rets, recv_sem=retr,
                device_id=(row, i), device_id_type=MESH,
            ).start()

        @pl.when(row != j)
        def _():
            for i in range(4):
                remote(i)

        @pl.when(row == j)
        def _():
            for i in range(4):

                @pl.when(s != i)
                def _(i=i):
                    remote(i)

                @pl.when(s == i)
                def _(i=i):
                    pltpu.make_async_copy(ret.at[4 * n + i], back.at[block], retr).start()

    def send_back_from(first, end):
        def body(n, _):
            send_back(n)
            return 0

        lax.fori_loop(first, end, body, 0)

    def await_terms(n):
        view = got.at[n, :, pl.ds(HALO - halo_of(n), B + 2 * halo_of(n)), :]
        pltpu.make_async_copy(view, view, gr.at[n]).wait()

    def hand_over(d):
        r = r_me + d + 8
        return pltpu.make_async_remote_copy(
            src_ref=s1.at[:, pl.ds(OFF + HALO, B), :], dst_ref=got.at[0, :, pl.ds(HALO - B * d, B), :],
            send_sem=hs.at[d + 1], recv_sem=gr.at[0],
            device_id=(chain_tm(1, lax.rem(r, 8)), lax.rem(s + r // 8 + 3, 4)), device_id_type=MESH,
        )

    @pl.when(is_worker)
    def _():
        for n in range(STEPS + 1):
            await_terms(n)
        for c in range(2):
            s0[c, pl.ds(OFF, GW), :] = got[0, c, :GW, :]
        pack(0, s0, OFF + HALO)
        for n in range(1, STEPS + 1):
            src, dst = (s0, s1) if n % 2 else (s1, s0)
            left = STEPS - n
            width = B + 4 * left
            heun(
                src, smid, dst, OFF + HALO - 2 * left, (width + 9) // 8, (width + 7) // 8, masks, COARSE,
                extra=lambda c, o, n=n: got[n, c, pl.ds(o - OFF, 8), :],
            )
            if n == STEPS:

                @pl.when(half == 0)
                def _():
                    for d in (-1, 0, 1):
                        hand_over(d).start()

            pack(n, dst, OFF + HALO)
            if n in BATCHES:
                first = max([m for m in BATCHES if m < n], default=0) + 1
                pl.when(half == 1)(lambda first=first, n=n: send_back_from(first, n + 1))

        pl.when(half == 0)(lambda: send_back_from(0, STEPS + 1))

    @pl.when(is_worker & (half == 0))
    def _():
        residual()

    @pl.when(j == 0)
    def _():
        for c in range(2):
            for t in range(2):
                turned = abuf[c, pl.ds(OFF + 64 + 128 * t, 128), :].T
                for i in range(4):
                    win[i, c, :, 128 * t : 128 * t + 128] = turned[32 * i : 32 * i + 32, :]
        coarse_ref[0, :, :, columns] = win[s, :, :, :256]
        copies = []
        for d in (1, 2, 3):
            to = lax.rem(s + d, 4)
            cp = pltpu.make_async_remote_copy(
                src_ref=win.at[to, :, :, pl.ds(0, 256)], dst_ref=coarse_ref.at[0, :, :, columns],
                send_sem=row0s.at[d - 1], recv_sem=row0r.at[d - 1], device_id=(j, to), device_id_type=MESH,
            )
            cp.start()
            copies.append(cp)
        for cp in copies:
            cp.wait()

    @pl.when(j > 0)
    def _():
        pltpu.make_async_copy(back, back, retr).wait()
        for c in range(2):
            for half in range(2):
                strips = []
                for e in range(4):
                    packed = [back[16 * half + 4 * k + e, c, :, :] for k in range(4)]
                    for g in range(4):
                        acc = None
                        for k in range(4):
                            amount = (32 * (k - g)) % 128
                            part = pltpu.roll(packed[k], amount, 1) if amount else packed[k]
                            acc = part if acc is None else jnp.where(group == k, part, acc)
                        strips.append(acc)
                square = jnp.concatenate(strips, axis=0).T
                for k in range(4):
                    tile = 4 * half + k
                    coarse_ref[0, c, :, 128 * tile : 128 * tile + 128] = square[32 * k : 32 * k + 32, :]

    pltpu.make_async_copy(resid_ref, resid_ref, resr).wait()
    for i in range(4):
        res_copy(i).wait_send()

    @pl.when(is_worker)
    def _():
        gather(finish)

    @pl.when(is_worker & (half == 0))
    def _():
        for d in (-1, 0, 1):
            hand_over(d).wait_send()

    for which, first, count in ((0, 0, 4 * STEPS + 4), (1, 4, 4 * STEPS)):

        @pl.when(is_worker & (half == which) & (lax.rem(j, 16) == 0))
        def _(first=first, count=count):
            view = ret.at[pl.ds(first, count)]
            pltpu.make_async_copy(view, view, rets).wait()

        @pl.when(is_worker & (half == which) & (lax.rem(j, 16) > 0))
        def _(first=first, count=count):
            view = ret.at[pl.ds(first, count - 1)]
            pltpu.make_async_copy(view, view, rets).wait()


def on_device(iterate):
    vmem = pl.BlockSpec(memory_space=pltpu.VMEM)
    dma = pltpu.SemaphoreType.DMA
    shape = jax.ShapeDtypeStruct((1, 2, 32, 1024), F32)
    coarse, resid = pl.pallas_call(
        kernel,
        out_shape=(shape, shape),
        in_specs=[pl.BlockSpec(memory_space=pl.ANY)],
        out_specs=(vmem, vmem),
        scratch_shapes=[
            pltpu.VMEM((2, 32, 1024), F32),
            pltpu.VMEM((2, 32, 1152), F32),
            pltpu.VMEM((4, 2, 32, WINDOW), F32),
            pltpu.VMEM((2, ROWS, 128), F32),
            pltpu.VMEM((2, ROWS, 128), F32),
            pltpu.VMEM((2, ROWS, 128), F32),
            pltpu.VMEM((2, ROWS, 128), F32),
            pltpu.VMEM((2, 256, 128), F32),
            pltpu.VMEM((2, 256, 128), F32),
            pltpu.VMEM((2, 256, 128), F32),
            pltpu.VMEM((STEPS + 1, 2, GW + 16, 128), F32),
            pltpu.VMEM((2, GW + 32, 128), F32),
            pltpu.VMEM((2, GW + 32, 128), F32),
            pltpu.VMEM((2, GW + 32, 128), F32),
            pltpu.VMEM((4 * STEPS + 4, 2, 8, 128), F32),
            pltpu.VMEM((32, 2, 8, 128), F32),
            pltpu.VMEM((4, 2, 32, 256), F32),
            dma, dma((3,)), dma((3,)),
            pltpu.SemaphoreType.REGULAR,
            dma, dma,
            dma((10,)), dma((STEPS + 1,)), dma((3,)),
            dma, dma,
            dma((4,)), dma,
            dma((3,)), dma((3,)),
        ],
        compiler_params=pltpu.CompilerParams(
            collective_id=0, has_side_effects=True, vmem_limit_bytes=48 * 2**20
        ),
    )(iterate)
    return coarse * (1.0 / SCALE), resid * (1.0 / SCALE)


def solution(mesh):
    spec = P("tm", None, "space", None)
    return jax.shard_map(on_device, mesh=mesh, in_specs=(spec,), out_specs=(spec, spec), check_vma=False)
```

time: 67.9 us -> 54.1 us (0.80)
  Pallas kernels: 64.8 us -> 51.3 us
  local copies, waits for them, and re-layouts: 2.35 us -> 0.94 us
  other arithmetic: 0 us -> 0.83 us
    pallas_call x1, Pallas kernels: 64.8 us -> 51.3 us  [on_device(): pl.pallas_call(kernel, out_shape=(shape, shape), in_specs=[pl.BlockSpec(m...]
    unnamed x4 -> x2, local copies, waits for them, and re-layouts: 2.35 us -> 0.94 us
    mul x0 -> x1, other arithmetic: none -> 0.83 us  [on_device(): return (coarse * (1.0 / SCALE), resid * (1.0 / SCALE))]
where the time goes in v2:
time: 54.1 us; the launch traced here: 53.7 us
  Pallas kernels  51.3 us (95%)
  local copies, waits for them, and re-layouts  0.94 us (2%)
  other arithmetic  0.83 us (2%)
  between operations  0.65 us (1%)
    pallas_call x1, Pallas kernels, on_device(): pl.pallas_call(kernel, out_shape=(shape, shape), in_specs=[pl.BlockSpec(m...  51.3 us

profile of v2, /device:TPU:25, one launch (start us, length us, event | category | flops | bytes accessed | tf_op | source)
XLA Modules:
  0.0 53.7 jit_solution(753483874769508059)
XLA Ops:
  0.6 0.0 copy-start
  0.6 0.9 %copy-done = f32[1,2,32,1024]{3,2,1,0:T(8,128)S(1)} copy-done((f32[1,2,32,1024]{3,2,1,0:T(8,128)S(1)}, f32[1,2,32,1024]{3,2,1,0:T(8,128)}, u32[]{:S(2)}) %copy-start) | copy-done | bytes 262168
  1.6 51.3 %shard_map.30 = (f32[1,2,32,1024]{3,2,1,0:T(8,128)S(1)}, f32[1,2,32,1024]{3,2,1,0:T(8,128)S(1)}) custom-call(f32[1,2,32,1024]{3,2,1,0:T(8,128)S(1)} %copy-done), custom_call_target="tpu_custom_call" | custom-call | tf_op jit(solution)/shard_map/pallas_call | solution.py:398
  52.8 0.8 %broadcast_multiply_fusion = (f32[1,2,32,1024]{3,2,1,0:T(8,128)}, f32[1,2,32,1024]{3,2,1,0:T(8,128)}) fusion(f32[1,2,32,1024]{3,2,1,0:T(8,128)S(1)} %get-tuple-element.5, f32[1,2,32,1024]{3,2,1,0:T(8,128)S(1)} %get-tuple-element.4), kind=kLoop, calls=%fused_computation | loop fusion | flops 131072 | bytes 1048576 | tf_op jit(solution)/shard_map/mul | solution.py:433
Async XLA Ops:
  0.6 1.0 %copy-start = (f32[1,2,32,1024]{3,2,1,0:T(8,128)S(1)}, f32[1,2,32,1024]{3,2,1,0:T(8,128)}, u32[]{:S(2)}) copy-start(f32[1,2,32,1024]{3,2,1,0:T(8,128)} %x_ref.1) | copy-start | bytes 786436

commit v3 on v2

--- a/solution.py
+++ b/solution.py
@@ -16,9 +16,9 @@
 OFF = 8
 ROWS = 432
 B = 32
-HALO = 32
-STEPS = 15
-BATCHES = (5, 10, 13, 15)
+STEPS = (15, 15)
+HALO = 8 * ((2 * max(STEPS) + 7) // 8)
+BATCHES = tuple(sorted({max(STEPS) - d for d in (0, 2, 5, 10, 15) if max(STEPS) > d}))
 GW = B + 2 * HALO
 
 
@@ -57,7 +57,7 @@
 
 
 def fine_steps(first, count, even, odd, mid, masks):
-    for g in range(first, first + count, 8):
+    for g in range(first, first + count, 4):
         n1 = (WINDOW - 2 - 4 * g + 7) // 8
         n2 = (WINDOW - 4 - 4 * g + 7) // 8
 
@@ -67,22 +67,27 @@
                 heun(src, mid, dst, start, n1, n2, masks, FINE)
             return 0
 
-        lax.fori_loop(g // 2, g // 2 + 4, body, 0)
-
-
-def halo_of(slot):
-    return 8 * ((2 * (STEPS - slot) + 7) // 8)
-
-
-def slot_classes():
-    edges = [n for n in range(STEPS + 1) if n == 0 or halo_of(n) != halo_of(n - 1)]
-    return [(n, m, halo_of(n)) for n, m in zip(edges, edges[1:] + [STEPS + 1])]
-
-
-def chain_tm(half, r):
-    y = r // 4 + half * (3 - 2 * (r // 4))
-    z = r // 4 * (7 - 2 * r) + r
-    return 8 * y + 2 * z
+        lax.fori_loop(g // 2, g // 2 + 2, body, 0)
+
+
+def halo_of(part, slot):
+    return 4 * ((2 * (STEPS[part] - slot) + 3) // 4)
+
+
+def slot_classes(part):
+    slots = range(part, STEPS[part] + 1)
+    edges = [n for n in slots if n == part or halo_of(part, n) != halo_of(part, n - 1)]
+    return [(n, m, halo_of(part, n)) for n, m in zip(edges, edges[1:] + [STEPS[part] + 1])]
+
+
+WORKERS = (
+    (0, 2, 4, 6, 14, 12, 10, 8),
+    (25, 27, 29, 31, 23, 21, 19, 17),
+)
+
+
+def pick(table, r):
+    return sum(jnp.where(r == i, tm, 0) for i, tm in enumerate(table))
 
 
 def kernel(
@@ -158,41 +163,40 @@
             coarse = jnp.where(j > 0, cbuf[c, rows, :], 0.0)
             terms[c, rows, :] = dbuf[c, pl.ds(OFF + 64 + 8 * i, 8), :] - coarse
 
-    half = j // 16
-    slot = j - STEPS * half
-
     def gather(act):
-        for first, end, h in slot_classes():
-
-            def pieces(h=h):
-                for r in range(-1, 9):
-                    lo, hi = max(0, B * r - h), min(256, B * r + B + h)
-                    if hi <= lo:
-                        continue
-                    src = terms.at[:, pl.ds(lo, hi - lo), :]
-                    dst = got.at[slot, :, pl.ds(lo - (B * r - HALO), hi - lo), :]
-                    holder = chain_tm(half, r % 8)
-                    to = lax.rem(s + (r // 8) + 4, 4)
-
-                    def remote(src=src, dst=dst, r=r, holder=holder, to=to):
-                        act(
-                            pltpu.make_async_remote_copy(
-                                src_ref=src, dst_ref=dst, send_sem=gs.at[r + 1], recv_sem=gr.at[slot],
-                                device_id=(holder, to), device_id_type=MESH,
-                            ),
-                            True,
-                        )
-
-                    if 0 <= r < 8:
-                        pl.when(j != holder)(remote)
-
-                        @pl.when(j == holder)
-                        def _(src=src, dst=dst):
-                            act(pltpu.make_async_copy(src, dst, gr.at[slot]), False)
-                    else:
-                        remote()
-
-            pl.when((slot >= first) & (slot < end))(pieces)
+        for part in range(2):
+            slot = j - STEPS[0] * part
+            for first, end, h in slot_classes(part):
+
+                def pieces(part=part, slot=slot, h=h):
+                    for r in range(-2, 10):
+                        lo, hi = max(0, B * r - h), min(256, B * r + B + h)
+                        if hi <= lo:
+                            continue
+                        src = terms.at[:, pl.ds(lo, hi - lo), :]
+                        dst = got.at[slot, :, pl.ds(lo - (B * r - HALO), hi - lo), :]
+                        holder = WORKERS[part][r % 8]
+                        to = lax.rem(s + (r // 8) + 4, 4)
+
+                        def remote(src=src, dst=dst, r=r, holder=holder, to=to):
+                            act(
+                                pltpu.make_async_remote_copy(
+                                    src_ref=src, dst_ref=dst, send_sem=gs.at[r + 2], recv_sem=gr.at[slot],
+                                    device_id=(holder, to), device_id_type=MESH,
+                                ),
+                                True,
+                            )
+
+                        if 0 <= r < 8:
+                            pl.when(j != holder)(remote)
+
+                            @pl.when(j == holder)
+                            def _(src=src, dst=dst):
+                                act(pltpu.make_async_copy(src, dst, gr.at[slot]), False)
+                        else:
+                            remote()
+
+                pl.when((slot >= first) & (slot < end))(pieces)
 
     def start(copy, remote):
         copy.start()
@@ -200,7 +204,8 @@
     gather(start)
 
     before.wait()
-    is_worker = lax.rem(j, 2) == 0
+    half = sum(jnp.where(j == tm, 1, 0) for tm in WORKERS[1])
+    is_worker = sum(jnp.where(j == tm, 1, 0) for tm in WORKERS[0] + WORKERS[1]) > 0
     columns = pl.ds(pl.multiple_of(256 * s, 128), 256)
 
     def residual():
@@ -232,7 +237,7 @@
     def _():
         residual()
 
-    r_me = 4 * jnp.where(half == 0, y, 3 - y) + jnp.where((y == 0) | (y == 3), q // 2, 3 - q // 2)
+    r_me = sum(jnp.where(j == tm, r, 0) for table in WORKERS for r, tm in enumerate(table))
     block = 8 * s + r_me
     group = lane // 32
 
@@ -247,8 +252,8 @@
                     acc = jnp.where(group == g, part, acc)
                 ret[4 * n + i, c, :, :] = acc
 
-    def send_back(n):
-        row = STEPS * half + n + 1
+    def send_back(part, n):
+        row = STEPS[0] * part + n + 1
 
         def remote(i):
             pltpu.make_async_remote_copy(
@@ -273,57 +278,89 @@
                 def _(i=i):
                     pltpu.make_async_copy(ret.at[4 * n + i], back.at[block], retr).start()
 
-    def send_back_from(first, end):
+    def send_back_from(part, first, end):
         def body(n, _):
-            send_back(n)
+            send_back(part, n)
             return 0
 
         lax.fori_loop(first, end, body, 0)
 
-    def await_terms(n):
-        view = got.at[n, :, pl.ds(HALO - halo_of(n), B + 2 * halo_of(n)), :]
+    def await_terms(part, n):
+        h = halo_of(part, n)
+        view = got.at[n, :, pl.ds(HALO - h, B + 2 * h), :]
         pltpu.make_async_copy(view, view, gr.at[n]).wait()
 
+    last_state = s1 if STEPS[0] % 2 else s0
+    first_h = halo_of(1, 0)
+
     def hand_over(d):
+        lo, hi = max(0, B * d - first_h), min(B, B * d + B + first_h)
         r = r_me + d + 8
         return pltpu.make_async_remote_copy(
-            src_ref=s1.at[:, pl.ds(OFF + HALO, B), :], dst_ref=got.at[0, :, pl.ds(HALO - B * d, B), :],
-            send_sem=hs.at[d + 1], recv_sem=gr.at[0],
-            device_id=(chain_tm(1, lax.rem(r, 8)), lax.rem(s + r // 8 + 3, 4)), device_id_type=MESH,
+            src_ref=last_state.at[:, pl.ds(OFF + HALO + lo, hi - lo), :],
+            dst_ref=got.at[0, :, pl.ds(HALO - B * d + lo, hi - lo), :],
+            send_sem=hs.at[d + 2], recv_sem=gr.at[0],
+            device_id=(pick(WORKERS[1], lax.rem(r, 8)), lax.rem(s + r // 8 + 3, 4)), device_id_type=MESH,
         )
 
-    @pl.when(is_worker)
-    def _():
-        for n in range(STEPS + 1):
-            await_terms(n)
+    near = [d for d in (-2, -1, 0, 1, 2) if abs(d) * B < B + first_h]
+
+    def chain(part):
+        for n in range(STEPS[part] + 1):
+            await_terms(part, n)
         for c in range(2):
             s0[c, pl.ds(OFF, GW), :] = got[0, c, :GW, :]
-        pack(0, s0, OFF + HALO)
-        for n in range(1, STEPS + 1):
+        if part == 0:
+            pack(0, s0, OFF + HALO)
+        for n in range(1, STEPS[part] + 1):
             src, dst = (s0, s1) if n % 2 else (s1, s0)
-            left = STEPS - n
+            left = STEPS[part] - n
             width = B + 4 * left
             heun(
                 src, smid, dst, OFF + HALO - 2 * left, (width + 9) // 8, (width + 7) // 8, masks, COARSE,
                 extra=lambda c, o, n=n: got[n, c, pl.ds(o - OFF, 8), :],
             )
-            if n == STEPS:
-
-                @pl.when(half == 0)
-                def _():
-                    for d in (-1, 0, 1):
-                        hand_over(d).start()
-
+            if part == 0 and n == STEPS[0]:
+                for d in near:
+                    hand_over(d).start()
             pack(n, dst, OFF + HALO)
-            if n in BATCHES:
-                first = max([m for m in BATCHES if m < n], default=0) + 1
-                pl.when(half == 1)(lambda first=first, n=n: send_back_from(first, n + 1))
-
-        pl.when(half == 0)(lambda: send_back_from(0, STEPS + 1))
+            if part == 1 and n in BATCHES:
+                send_back_from(1, max([m for m in BATCHES if m < n], default=0) + 1, n + 1)
+        if part == 0:
+            send_back_from(0, 0, STEPS[0] + 1)
+
+    for which in range(2):
+        pl.when(is_worker & (half == which))(lambda which=which: chain(which))
 
     @pl.when(is_worker & (half == 0))
     def _():
         residual()
+
+    pltpu.make_async_copy(resid_ref, resid_ref, resr).wait()
+    for i in range(4):
+        res_copy(i).wait_send()
+
+    @pl.when(is_worker)
+    def _():
+        gather(finish)
+
+    @pl.when(is_worker & (half == 0))
+    def _():
+        for d in near:
+            hand_over(d).wait_send()
+
+    for which, first, count in ((0, 0, 4 * STEPS[0] + 4), (1, 4, 4 * STEPS[1])):
+        inside = (j > 0) & (j < STEPS[0] + 2) if which == 0 else j > STEPS[0] + 1
+
+        @pl.when(is_worker & (half == which) & inside)
+        def _(first=first, count=count):
+            view = ret.at[pl.ds(first, count - 1)]
+            pltpu.make_async_copy(view, view, rets).wait()
+
+        @pl.when(is_worker & (half == which) & jnp.logical_not(inside))
+        def _(first=first, count=count):
+            view = ret.at[pl.ds(first, count)]
+            pltpu.make_async_copy(view, view, rets).wait()
 
     @pl.when(j == 0)
     def _():
@@ -364,31 +401,6 @@
                 for k in range(4):
                     tile = 4 * half + k
                     coarse_ref[0, c, :, 128 * tile : 128 * tile + 128] = square[32 * k : 32 * k + 32, :]
-
-    pltpu.make_async_copy(resid_ref, resid_ref, resr).wait()
-    for i in range(4):
-        res_copy(i).wait_send()
-
-    @pl.when(is_worker)
-    def _():
-        gather(finish)
-
-    @pl.when(is_worker & (half == 0))
-    def _():
-        for d in (-1, 0, 1):
-            hand_over(d).wait_send()
-
-    for which, first, count in ((0, 0, 4 * STEPS + 4), (1, 4, 4 * STEPS)):
-
-        @pl.when(is_worker & (half == which) & (lax.rem(j, 16) == 0))
-        def _(first=first, count=count):
-            view = ret.at[pl.ds(first, count)]
-            pltpu.make_async_copy(view, view, rets).wait()
-
-        @pl.when(is_worker & (half == which) & (lax.rem(j, 16) > 0))
-        def _(first=first, count=count):
-            view = ret.at[pl.ds(first, count - 1)]
-            pltpu.make_async_copy(view, view, rets).wait()
 
 
 def on_device(iterate):
@@ -411,17 +423,17 @@
             pltpu.VMEM((2, 256, 128), F32),
             pltpu.VMEM((2, 256, 128), F32),
             pltpu.VMEM((2, 256, 128), F32),
-            pltpu.VMEM((STEPS + 1, 2, GW + 16, 128), F32),
+            pltpu.VMEM((max(STEPS) + 1, 2, GW + 16, 128), F32),
             pltpu.VMEM((2, GW + 32, 128), F32),
             pltpu.VMEM((2, GW + 32, 128), F32),
             pltpu.VMEM((2, GW + 32, 128), F32),
-            pltpu.VMEM((4 * STEPS + 4, 2, 8, 128), F32),
+            pltpu.VMEM((4 * max(STEPS) + 4, 2, 8, 128), F32),
             pltpu.VMEM((32, 2, 8, 128), F32),
             pltpu.VMEM((4, 2, 32, 256), F32),
             dma, dma((3,)), dma((3,)),
             pltpu.SemaphoreType.REGULAR,
             dma, dma,
-            dma((10,)), dma((STEPS + 1,)), dma((3,)),
+            dma((12,)), dma((max(STEPS) + 1,)), dma((5,)),
             dma, dma,
             dma((4,)), dma,
             dma((3,)), dma((3,)),

time: 54.1 us -> 52.1 us (0.963)
  Pallas kernels: 51.3 us -> 49.5 us
    pallas_call x1, Pallas kernels: 51.3 us -> 49.5 us  [on_device(): pl.pallas_call(kernel, out_shape=(shape, shape), in_specs=[pl.BlockSpec(m...]
where the time goes in v3:
time: 52.1 us; the launch traced here: 52 us
  Pallas kernels  49.5 us (95%)
  local copies, waits for them, and re-layouts  0.94 us (2%)
  other arithmetic  0.83 us (2%)
  between operations  0.65 us (1%)
    pallas_call x1, Pallas kernels, on_device(): pl.pallas_call(kernel, out_shape=(shape, shape), in_specs=[pl.BlockSpec(m...  49.5 us

profile of v3, /device:TPU:25, one launch (start us, length us, event | category | flops | bytes accessed | tf_op | source)
XLA Modules:
  0.0 52.0 jit_solution(17162419768611235675)
XLA Ops:
  0.6 0.0 copy-start
  0.6 0.9 %copy-done = f32[1,2,32,1024]{3,2,1,0:T(8,128)S(1)} copy-done((f32[1,2,32,1024]{3,2,1,0:T(8,128)S(1)}, f32[1,2,32,1024]{3,2,1,0:T(8,128)}, u32[]{:S(2)}) %copy-start) | copy-done | bytes 262168
  1.6 49.5 %shard_map.30 = (f32[1,2,32,1024]{3,2,1,0:T(8,128)S(1)}, f32[1,2,32,1024]{3,2,1,0:T(8,128)S(1)}) custom-call(f32[1,2,32,1024]{3,2,1,0:T(8,128)S(1)} %copy-done), custom_call_target="tpu_custom_call" | custom-call | tf_op jit(solution)/shard_map/pallas_call | solution.py:410
  51.1 0.8 %broadcast_multiply_fusion = (f32[1,2,32,1024]{3,2,1,0:T(8,128)}, f32[1,2,32,1024]{3,2,1,0:T(8,128)}) fusion(f32[1,2,32,1024]{3,2,1,0:T(8,128)S(1)} %get-tuple-element.5, f32[1,2,32,1024]{3,2,1,0:T(8,128)S(1)} %get-tuple-element.4), kind=kLoop, calls=%fused_computation | loop fusion | flops 131072 | bytes 1048576 | tf_op jit(solution)/shard_map/mul | solution.py:445
Async XLA Ops:
  0.6 1.0 %copy-start = (f32[1,2,32,1024]{3,2,1,0:T(8,128)S(1)}, f32[1,2,32,1024]{3,2,1,0:T(8,128)}, u32[]{:S(2)}) copy-start(f32[1,2,32,1024]{3,2,1,0:T(8,128)} %x_ref.1) | copy-start | bytes 786436

commit v4 on v3

--- a/solution.py
+++ b/solution.py
@@ -257,7 +257,7 @@
 
         def remote(i):
             pltpu.make_async_remote_copy(
-                src_ref=ret.at[4 * n + i], dst_ref=back.at[block], send_sem=rets, recv_sem=retr,
+                src_ref=ret.at[4 * n + i], dst_ref=back.at[block], send_sem=rets, recv_sem=retr.at[s // 2],
                 device_id=(row, i), device_id_type=MESH,
             ).start()
 
@@ -276,7 +276,7 @@
 
                 @pl.when(s == i)
                 def _(i=i):
-                    pltpu.make_async_copy(ret.at[4 * n + i], back.at[block], retr).start()
+                    pltpu.make_async_copy(ret.at[4 * n + i], back.at[block], retr.at[s // 2]).start()
 
     def send_back_from(part, first, end):
         def body(n, _):
@@ -306,7 +306,7 @@
     near = [d for d in (-2, -1, 0, 1, 2) if abs(d) * B < B + first_h]
 
     def chain(part):
-        for n in range(STEPS[part] + 1):
+        for n in list(range(1, STEPS[part] + 1)) + [0]:
             await_terms(part, n)
         for c in range(2):
             s0[c, pl.ds(OFF, GW), :] = got[0, c, :GW, :]
@@ -384,12 +384,14 @@
 
     @pl.when(j > 0)
     def _():
-        pltpu.make_async_copy(back, back, retr).wait()
-        for c in range(2):
-            for half in range(2):
+        for turn in range(2):
+            half_at = lax.rem(s // 2 + turn, 2)
+            view = back.at[pl.ds(16 * half_at, 16)]
+            pltpu.make_async_copy(view, view, retr.at[half_at]).wait()
+            for c in range(2):
                 strips = []
                 for e in range(4):
-                    packed = [back[16 * half + 4 * k + e, c, :, :] for k in range(4)]
+                    packed = [back[16 * half_at + 4 * k + e, c, :, :] for k in range(4)]
                     for g in range(4):
                         acc = None
                         for k in range(4):
@@ -399,8 +401,8 @@
                         strips.append(acc)
                 square = jnp.concatenate(strips, axis=0).T
                 for k in range(4):
-                    tile = 4 * half + k
-                    coarse_ref[0, c, :, 128 * tile : 128 * tile + 128] = square[32 * k : 32 * k + 32, :]
+                    tile = pl.ds(pl.multiple_of(512 * half_at + 128 * k, 128), 128)
+                    coarse_ref[0, c, :, tile] = square[32 * k : 32 * k + 32, :]
 
 
 def on_device(iterate):
@@ -434,7 +436,7 @@
             pltpu.SemaphoreType.REGULAR,
             dma, dma,
             dma((12,)), dma((max(STEPS) + 1,)), dma((5,)),
-            dma, dma,
+            dma, dma((2,)),
             dma((4,)), dma,
             dma((3,)), dma((3,)),
         ],

time: 52.1 us -> 52.2 us (level)
  no operation moved by 1% of the time
where the time goes in v4:
time: 52.2 us; the launch traced here: 52.1 us
  Pallas kernels  49.6 us (95%)
  local copies, waits for them, and re-layouts  0.94 us (2%)
  other arithmetic  0.83 us (2%)
  between operations  0.65 us (1%)
    pallas_call x1, Pallas kernels, on_device(): pl.pallas_call(kernel, out_shape=(shape, shape), in_specs=[pl.BlockSpec(m...  49.6 us

profile of v4, /device:TPU:25, one launch (start us, length us, event | category | flops | bytes accessed | tf_op | source)
XLA Modules:
  0.0 52.1 jit_solution(2837416837937099871)
XLA Ops:
  0.6 0.0 copy-start
  0.6 0.9 %copy-done = f32[1,2,32,1024]{3,2,1,0:T(8,128)S(1)} copy-done((f32[1,2,32,1024]{3,2,1,0:T(8,128)S(1)}, f32[1,2,32,1024]{3,2,1,0:T(8,128)}, u32[]{:S(2)}) %copy-start) | copy-done | bytes 262168
  1.6 49.6 %shard_map.30 = (f32[1,2,32,1024]{3,2,1,0:T(8,128)S(1)}, f32[1,2,32,1024]{3,2,1,0:T(8,128)S(1)}) custom-call(f32[1,2,32,1024]{3,2,1,0:T(8,128)S(1)} %copy-done), custom_call_target="tpu_custom_call" | custom-call | tf_op jit(solution)/shard_map/pallas_call | solution.py:412
  51.2 0.8 %broadcast_multiply_fusion = (f32[1,2,32,1024]{3,2,1,0:T(8,128)}, f32[1,2,32,1024]{3,2,1,0:T(8,128)}) fusion(f32[1,2,32,1024]{3,2,1,0:T(8,128)S(1)} %get-tuple-element.5, f32[1,2,32,1024]{3,2,1,0:T(8,128)S(1)} %get-tuple-element.4), kind=kLoop, calls=%fused_computation | loop fusion | flops 131072 | bytes 1048576 | tf_op jit(solution)/shard_map/mul | solution.py:447
Async XLA Ops:
  0.6 1.0 %copy-start = (f32[1,2,32,1024]{3,2,1,0:T(8,128)S(1)}, f32[1,2,32,1024]{3,2,1,0:T(8,128)}, u32[]{:S(2)}) copy-start(f32[1,2,32,1024]{3,2,1,0:T(8,128)} %x_ref.1) | copy-start | bytes 786436
